TPU v7x, 32 devices: a whole 2x2x4 slice. The times are simulated.
32 devices in a mesh: tm: 4 (over y, x), space: 8 (over z, core).
Axes of the slice: x: 2, y: 2, z: 4, core: 2. Of those that a mesh axis runs over, the one named last changes fastest.
Arguments:
- latent_clip: bfloat16 [8, 16, 32, 256], P('tm', 'space'), may hold values from -45 to 45
- cotangent: bfloat16 [8, 16, 32, 128], P('tm', 'space'), may hold values from -6 to 6
- conv_weight: bfloat16 [6912, 128], replicated, may hold values from -0.078125 to 0.078125
- norm_gain: float32 [256], replicated, may hold values from 0.5 to 1.5
- norm_shift: float32 [256], replicated, may hold values from -2 to 2
Outputs:
- clip_grad: bfloat16 [8, 16, 32, 256], P('tm', 'space')
- weight_grad: float32 [6912, 128], P('space')
- gain_grad: float32 [256], replicated
- shift_grad: float32 [256], replicated
All inputs are finite; a program needn't handle non-finite values.
Results may differ from a plain program's by a relative error of at most 0.0029.
Values may be sent and summed in bfloat16 or wider, within the bound.
A program may use at most 64 MiB of HBM per device.

v0:
```python
import jax
import jax.numpy as jnp
from jax import lax
from jax.sharding import PartitionSpec as P

GROUPS = 32


def shifted(value, axis, steps):
    count = lax.axis_size(axis)
    leading, last = (max(0, -steps), min(count, count - steps))
    return lax.ppermute(value, axis, [(source, source + steps) for source in range(leading, last)])


def extended_2(block, sides, width):
    for axis, dim in sides:
        count = lax.axis_size(axis)
        forward = [(i, i + 1) for i in range(count - 1)]
        backward = [(target, source) for source, target in forward]
        low = lax.ppermute(
            lax.slice_in_dim(block, block.shape[dim] - width, None, axis=dim), axis, forward
        )
        high = lax.ppermute(lax.slice_in_dim(block, 0, width, axis=dim), axis, backward)
        block = jnp.concatenate([low, block, high], axis=dim)
    return block


def silu_slope(activation):
    sigma = jax.nn.sigmoid(activation)
    return sigma * (1.0 + activation * (1.0 - sigma))


def tap_block(source, anchors, frame_count, row_count, col_count):
    pieces = [
        source[
            anchor[0] : anchor[0] + frame_count,
            anchor[1] : anchor[1] + row_count,
            anchor[2] : anchor[2] + col_count,
            :,
        ]
        for anchor in anchors
    ]
    merged = jnp.concatenate(pieces, axis=-1)
    return merged.reshape(frame_count * row_count * col_count, merged.shape[-1])


def transposed(grad_pad, conv_weight, frame_count, row_count, col_count):
    out_channels = conv_weight.shape[1]
    channels = conv_weight.shape[0] // 27
    kernel = conv_weight.reshape(3, 3, 3, channels, out_channels)
    total = jnp.zeros((frame_count * row_count * col_count, channels), jnp.float32)
    for tap_time in range(3):
        anchors = [
            (2 - tap_time, 2 - tap_row, 2 - tap_col) for tap_row in range(3) for tap_col in range(3)
        ]
        tap_cols = tap_block(grad_pad, anchors, frame_count, row_count, col_count)
        flipped = jnp.transpose(kernel[tap_time], (0, 1, 3, 2)).reshape(9 * out_channels, channels)
        total = total + jnp.dot(tap_cols, flipped, preferred_element_type=jnp.float32)
    return total.reshape(frame_count, row_count, col_count, channels)


def shards(latent_clip, cotangent, conv_weight, norm_gain, norm_shift):
    frame_count, row_count, col_count, channels = latent_clip.shape
    out_channels = cotangent.shape[-1]
    width_group = channels // GROUPS
    tm_size = lax.axis_size("tm")
    space_size = lax.axis_size("space")
    group_count = frame_count * row_count * col_count * width_group * tm_size * space_size
    values = latent_clip.astype(jnp.float32).reshape(
        frame_count, row_count, col_count, GROUPS, width_group
    )
    group_mean = lax.psum(jnp.sum(values, axis=(0, 1, 2, 4)), ("tm", "space")) / group_count
    centered = values - group_mean[:, None]
    group_var = (
        lax.psum(jnp.sum(centered * centered, axis=(0, 1, 2, 4)), ("tm", "space")) / group_count
    )
    inv_std = lax.rsqrt(group_var + 1e-06)
    normed = (centered * inv_std[:, None]).reshape(frame_count, row_count, col_count, channels)
    activation = normed * norm_gain + norm_shift
    hidden = jax.nn.silu(activation).astype(jnp.bfloat16)
    ahead = shifted(cotangent, "tm", -1)
    time_source = jnp.concatenate([cotangent, ahead], axis=0)
    time_pad = (0, 0)
    cached = shifted(hidden, "tm", 1)
    extended = jnp.concatenate([cached, hidden], axis=0)
    rimmed = extended_2(extended, (("space", 1),), 1)
    padded = jnp.pad(rimmed, ((0, 0), (0, 0), (1, 1), (0, 0)))
    cell_count = frame_count * row_count * col_count
    upstream = cotangent.reshape(cell_count, out_channels)
    tap_grads = []
    for tap_time in range(3):
        anchors = [(tap_time, tap_row, tap_col) for tap_row in range(3) for tap_col in range(3)]
        tap_cols = tap_block(padded, anchors, frame_count, row_count, col_count)
        tap_grads.append(
            lax.dot_general(
                tap_cols, upstream, (((0,), (0,)), ((), ())), preferred_element_type=jnp.float32
            )
        )
    local_grad = jnp.concatenate(tap_grads, axis=0)
    space_shard = lax.psum_scatter(local_grad, "space", scatter_dimension=0, tiled=True)
    weight_grad = lax.psum(space_shard, "tm")
    grad_pad = jnp.pad(time_source, (time_pad, (2, 2), (1, 1), (0, 0)))
    spread = transposed(grad_pad, conv_weight, frame_count, row_count + 2, col_count)
    from_below = shifted(spread[:, 0], "space", -1)
    from_above = shifted(spread[:, row_count + 1], "space", 1)
    inner = spread[:, 1 : row_count + 1]
    inner = inner.at[:, row_count - 1].add(from_below)
    inner = inner.at[:, 0].add(from_above)
    activation_grad = inner * silu_slope(activation)
    gain_grad, shift_grad = lax.psum(
        (
            jnp.sum(activation_grad * normed, axis=(0, 1, 2)),
            jnp.sum(activation_grad, axis=(0, 1, 2)),
        ),
        ("tm", "space"),
    )
    first = jnp.sum((norm_gain * shift_grad).reshape(GROUPS, width_group), axis=1)
    second = jnp.sum((norm_gain * gain_grad).reshape(GROUPS, width_group), axis=1)
    scaled = (activation_grad * norm_gain).reshape(
        frame_count, row_count, col_count, GROUPS, width_group
    )
    normed_groups = normed.reshape(frame_count, row_count, col_count, GROUPS, width_group)
    clip_grad = inv_std[:, None] * (
        scaled - first[:, None] / group_count - normed_groups * second[:, None] / group_count
    )
    clip_grad = clip_grad.reshape(frame_count, row_count, col_count, channels).astype(jnp.bfloat16)
    return (clip_grad, weight_grad, gain_grad, shift_grad)


def solution(mesh):
    return jax.shard_map(
        shards,
        mesh=mesh,
        in_specs=(P("tm", "space", None, None), P("tm", "space", None, None), P(), P(), P()),
        out_specs=(P("tm", "space", None, None), P("space", None), P(), P()),
        check_vma=False,
    )
```

profile of v0, /device:TPU:0, one launch (start us, length us, event | category | flops | bytes accessed | tf_op | source)
XLA Modules:
  0.0 225.5 jit_solution(13261450040164895884)
XLA Ops:
  7.2 0.9 convert_reduce_fusion
  8.1 0.1 reduce_sum.69
  8.2 0.1 reduce_sum.70
  8.3 1.3 collective-permute-start
  9.6 43.2 %psum.35 = f32[32]{0:T(128)S(1)} all-reduce(f32[32]{0:T(128)S(1)} %reduce_sum.70), channel_id=1, replica_groups=mesh['tm'=4,'space'=8] {'tm','space'}, use_global_device_ids=true, to_apply=%region_2.0 | all-reduce | flops 32 | bytes 256 | tf_op jit(solution)/shard_map/psum | solution.py:72
  52.8 0.1 sub.35
  52.8 0.1 sub.36
  52.9 0.9 fusion.33
  53.8 0.1 reduce_sum.72
  53.9 0.1 reduce_sum.73
  54.0 1.5 fusion.40
  55.6 41.0 %psum.36 = f32[32]{0:T(128)S(1)} all-reduce(f32[32]{0:T(128)S(1)} %reduce_sum.73), channel_id=1, replica_groups=mesh['tm'=4,'space'=8] {'tm','space'}, use_global_device_ids=true, to_apply=%region_5.6 | all-reduce | flops 32 | bytes 256 | tf_op jit(solution)/shard_map/psum | solution.py:75
  96.6 0.2 copy.15
  96.8 0.2 copy.13
  97.1 0.2 copy.14
  97.3 0.2 copy-done.1
  97.8 0.1 constant_dynamic-update-slice_fusion.23
  98.0 0.1 constant_dynamic-update-slice_fusion.20
  98.1 0.1 constant_dynamic-update-slice_fusion.19
  98.3 0.3 fusion.42
  98.6 0.3 convolution_add_fusion.1
  99.0 0.3 convolution_add_fusion
  99.4 1.3 collective-permute-start.1
  100.8 0.1 mul.76
  100.9 3.0 %collective-permute-start.2 = (f32[2,32,256]{2,1,0:T(8,128)S(1)}, f32[2,32,256]{2,1,0:T(8,128)S(1)}, u32[]{:S(2)}, u32[]{:S(2)}) collective-permute-start(f32[2,32,256]{2,1,0:T(8,128)S(1)} %get-tuple-element.53), channel_id=1, source_target_pairs={{0,1},{1,2},{2,3},{3,4},{4,5},{5,6},{6,7},{8,9},{9,10},{10,11},{11... | collective-permute-start | bytes 196616 | tf_op jit(solution)/shard_map/ppermute | solution.py:12
  103.9 0.9 collective-permute-done.2
  104.8 0.1 fusion.38
  105.0 4.2 %collective-permute-start.3 = (bf16[2,2,32,256]{3,2,1,0:T(8,128)(2,1)S(1)}, bf16[2,2,32,256]{3,2,1,0:T(8,128)(2,1)S(1)}, u32[]{:S(2)}, u32[]{:S(2)}) collective-permute-start(bf16[2,2,32,256]{3,2,1,0:T(8,128)(2,1)S(1)} %get-tuple-element.90), channel_id=1, source_target_pairs={{0,8},{8,16},{16,24},{1,9},{9,17},{17,25},{2,10},{10,18},{18,26},{... | collective-permute-start | bytes 196616 | tf_op jit(solution)/shard_map/ppermute | solution.py:12
  109.1 1.9 collective-permute-done.3
  111.1 1.4 collective-permute-start.4
  112.6 1.3 collective-permute-start.5
  113.9 4.6 %collective-permute-done.5 = bf16[4,1,32,256]{3,2,1,0:T(8,128)(2,1)S(1)} collective-permute-done((bf16[4,1,32,256]{3,2,1,0:T(8,128)(2,1)S(1)}, bf16[4,1,32,256]{3,2,1,0:T(8,128)(2,1)S(1)}, u32[]{:S(2)}, u32[]{:S(2)}) %collective-permute-start.5) | collective-permute-done | bytes 65568 | tf_op jit(solution)/shard_map/ppermute | solution.py:23
  118.4 0.1 select_maximum_fusion
  118.9 0.3 convolution_bitcast_fusion
  119.2 0.3 convolution_bitcast_fusion.2
  119.6 0.3 convolution_bitcast_fusion.1
  119.9 2.0 pad_maximum_fusion
  122.0 45.1 %all-reduce.2 = (f32[256]{0:T(256)S(1)}, f32[256]{0:T(256)S(1)}) all-reduce(f32[256]{0:T(256)S(1)} %get-tuple-element.29, f32[256]{0:T(256)S(1)} %get-tuple-element.28), channel_id=1, replica_groups=mesh['tm'=4,'space'=8] {'tm','space'}, use_global_device_ids=true, to_apply=%region_10.11 | all-reduce | flops 512 | bytes 4096 | tf_op jit(solution)/shard_map/psum | solution.py:110
  167.2 0.1 reshape.151
  167.2 0.1 reduce_sum.75
  167.4 3.1 %reduce-scatter.2.cloned.1.call-done = f32[864,128]{1,0:T(8,128)} async-done(((f32[6912,128]{1,0:T(8,128)}), f32[864,128]{1,0:T(8,128)}) %reduce-scatter.2.cloned.1.call-update) | async-done | bytes 442384 | tf_op jit(solution)/shard_map/reduce_scatter | solution.py:100
  170.6 0.1 sub.41
  170.7 0.1 reshape.152
  170.8 0.1 reduce_sum.77
  171.0 0.1 mul.89
  171.1 0.7 fusion.32
  171.8 45.1 %all-reduce.5.cloned.1.call-done = f32[864,128]{1,0:T(8,128)} async-done(((f32[864,128]{1,0:T(8,128)}), f32[864,128]{1,0:T(8,128)}) %all-reduce.5.cloned.1.call-update) | async-done | bytes 442384 | tf_op jit(solution)/shard_map/psum | solution.py:101
  216.9 1.8 copy.74
  (51 shorter events, 1.1 us)
Async XLA Ops:
  7.2 163.3 %reduce-scatter.2.cloned.1.call-start = ((), (), s32[]{:S(2)}) async-start(), calls=%async_computation.1 | async-start | bytes 3981312 | tf_op jit(solution)/shard_map/reduce_scatter | solution.py:100
  8.3 89.0 %collective-permute-start = (bf16[2,2,32,128]{3,2,1,0:T(8,128)(2,1)}, bf16[2,2,32,128]{3,2,1,0:T(8,128)(2,1)S(1)}, u32[]{:S(2)}, u32[]{:S(2)}) collective-permute-start(bf16[2,2,32,128]{3,2,1,0:T(8,128)(2,1)} %param.10), channel_id=1, source_target_pairs={{8,0},{16,8},{24,16},{9,1},{17,9},{25,17},{10,2},{18,10},{26,18},{... | collective-permute-start | bytes 98312 | tf_op jit(solution)/shard_map/ppermute | solution.py:12
  96.8 0.8 copy-start.1
  99.0 5.8 %copy-start = (bf16[2,2,32,256]{3,2,1,0:T(8,128)(2,1)S(1)}, bf16[2,2,32,256]{3,2,1,0:T(8,128)(2,1)}, u32[]{:S(2)}) copy-start(bf16[2,2,32,256]{3,2,1,0:T(8,128)(2,1)} %param.9) | copy-start | bytes 196612
  99.0 5.8 %copy-start.2 = (f32[256]{0:T(256)S(1)}, f32[256]{0:T(256)}, u32[]{:S(2)}) copy-start(f32[256]{0:T(256)} %param.12) | copy-start | bytes 3076
  99.0 5.8 %copy-start.3 = (f32[256]{0:T(256)S(1)}, f32[256]{0:T(256)}, u32[]{:S(2)}) copy-start(f32[256]{0:T(256)} %param.13) | copy-start | bytes 3076
  99.4 4.5 %collective-permute-start.1 = (f32[2,32,256]{2,1,0:T(8,128)S(1)}, f32[2,32,256]{2,1,0:T(8,128)S(1)}, u32[]{:S(2)}, u32[]{:S(2)}) collective-permute-start(f32[2,32,256]{2,1,0:T(8,128)S(1)} %get-tuple-element.54), channel_id=1, source_target_pairs={{1,0},{2,1},{3,2},{4,3},{5,4},{6,5},{7,6},{9,8},{10,9},{11,10},{12... | collective-permute-start | bytes 196616 | tf_op jit(solution)/shard_map/ppermute | solution.py:12
  100.9 3.9 %collective-permute-start.2 = (f32[2,32,256]{2,1,0:T(8,128)S(1)}, f32[2,32,256]{2,1,0:T(8,128)S(1)}, u32[]{:S(2)}, u32[]{:S(2)}) collective-permute-start(f32[2,32,256]{2,1,0:T(8,128)S(1)} %get-tuple-element.53), channel_id=1, source_target_pairs={{0,1},{1,2},{2,3},{3,4},{4,5},{5,6},{6,7},{8,9},{9,10},{10,11},{11... | collective-permute-start | bytes 196616 | tf_op jit(solution)/shard_map/ppermute | solution.py:12
  105.0 6.1 %collective-permute-start.3 = (bf16[2,2,32,256]{3,2,1,0:T(8,128)(2,1)S(1)}, bf16[2,2,32,256]{3,2,1,0:T(8,128)(2,1)S(1)}, u32[]{:S(2)}, u32[]{:S(2)}) collective-permute-start(bf16[2,2,32,256]{3,2,1,0:T(8,128)(2,1)S(1)} %get-tuple-element.90), channel_id=1, source_target_pairs={{0,8},{8,16},{16,24},{1,9},{9,17},{17,25},{2,10},{10,18},{18,26},{... | collective-permute-start | bytes 196616 | tf_op jit(solution)/shard_map/ppermute | solution.py:12
  111.1 2.8 %collective-permute-start.4 = (bf16[4,1,32,256]{3,2,1,0:T(8,128)(2,1)S(1)}, bf16[4,1,32,256]{3,2,1,0:T(8,128)(2,1)S(1)}, u32[]{:S(2)}, u32[]{:S(2)}) collective-permute-start(bf16[4,1,32,256]{3,2,1,0:T(8,128)(2,1)S(1)} %get-tuple-element.88), channel_id=1, source_target_pairs={{0,1},{1,2},{2,3},{3,4},{4,5},{5,6},{6,7},{8,9},{9,10},{10,11},{11... | collective-permute-start | bytes 196616 | tf_op jit(solution)/shard_map/ppermute | solution.py:20
  112.6 5.9 %collective-permute-start.5 = (bf16[4,1,32,256]{3,2,1,0:T(8,128)(2,1)S(1)}, bf16[4,1,32,256]{3,2,1,0:T(8,128)(2,1)S(1)}, u32[]{:S(2)}, u32[]{:S(2)}) collective-permute-start(bf16[4,1,32,256]{3,2,1,0:T(8,128)(2,1)S(1)} %get-tuple-element.89), channel_id=1, source_target_pairs={{1,0},{2,1},{3,2},{4,3},{5,4},{6,5},{7,6},{9,8},{10,9},{11,10},{12... | collective-permute-start | bytes 196616 | tf_op jit(solution)/shard_map/ppermute | solution.py:23
  122.0 94.9 %all-reduce.5.cloned.1.call-start = ((), (), s32[]{:S(2)}) async-start(), calls=%async_computation.2 | async-start | bytes 884736 | tf_op jit(solution)/shard_map/psum | solution.py:101
  167.2 51.5 %copy-start.4 = (f32[256]{0:T(256)}, f32[256]{0:T(256)S(1)}, u32[]{:S(2)}) copy-start(f32[256]{0:T(256)S(1)} %get-tuple-element.97) | copy-start | bytes 3076
  167.2 51.5 %copy-start.5 = (f32[256]{0:T(256)}, f32[256]{0:T(256)S(1)}, u32[]{:S(2)}) copy-start(f32[256]{0:T(256)S(1)} %get-tuple-element.98) | copy-start | bytes 3076
Sparse Core Ops, SparseCore 0:
  122.1 48.3 reduce-scatter.1
  173.8 43.0 all-reduce.4
where the time goes:
time: 226 us
  blocking collectives  129 us (57%)
  waiting for transfers between devices  55.6 us (25%)
  between operations  14.5 us (6%)
  starting transfers between devices  12.6 us (6%)
  local copies, waits for them, and re-layouts  6.15 us (3%)
  other arithmetic  5.25 us (2%)
    psum x1, blocking collectives, shards(): lax.psum((jnp.sum(activation_grad * normed, axis=(0, 1, 2)), jnp.sum(acti...  45.1 us
    psum x1, waiting for transfers between devices, shards(): weight_grad = lax.psum(space_shard, 'tm')  45.1 us
    psum x1, blocking collectives, shards(): lax.psum(jnp.sum(values, axis=(0, 1, 2, 4)), ('tm', 'space')) / group_count  43.2 us
    psum x1, blocking collectives, shards(): lax.psum(jnp.sum(centered * centered, axis=(0, 1, 2, 4)), ('tm', 'space'))  41 us
    ppermute x4, starting transfers between devices, shifted(): lax.ppermute(value, axis, [(source, source + steps) for source in range(l...  9.8 us
    ppermute x1, waiting for transfers between devices, extended_2(): lax.ppermute(lax.slice_in_dim(block, 0, width, axis=dim), axis, backward)  4.55 us
  transfers between devices with their start and end apart: 8, of which 5 were waited for; matrix products, arithmetic and copies ran while one was open for 2% of the time, Pallas kernels for 0%

commit v1 on v0

--- a/solution.py
+++ b/solution.py
@@ -98,7 +98,7 @@
         )
     local_grad = jnp.concatenate(tap_grads, axis=0)
     space_shard = lax.psum_scatter(local_grad, "space", scatter_dimension=0, tiled=True)
-    weight_grad = lax.psum(space_shard, "tm")
+    weight_grad = jnp.sum(lax.all_gather(space_shard, "tm"), axis=0)
     grad_pad = jnp.pad(time_source, (time_pad, (2, 2), (1, 1), (0, 0)))
     spread = transposed(grad_pad, conv_weight, frame_count, row_count + 2, col_count)
     from_below = shifted(spread[:, 0], "space", -1)

time: 226 us -> 219 us (0.969)
  blocking collectives: 129 us -> 122 us
  other arithmetic: 5.25 us -> 7.62 us
    psum x1 -> x0, waiting for transfers between devices: 45.1 us -> none  [shards(): weight_grad = lax.psum(space_shard, 'tm')]
    reduce_scatter x1, waiting for transfers between devices: 3.13 us -> 47.5 us  [shards(): lax.psum_scatter(local_grad, 'space', scatter_dimension=0, tiled=True)]
    psum x1, blocking collectives: 45.1 us -> 38.1 us  [shards(): lax.psum((jnp.sum(activation_grad * normed, axis=(0, 1, 2)), jnp.sum(acti...]
    reduce_sum x0 -> x1, other arithmetic: none -> 2.38 us  [shards(): weight_grad = jnp.sum(lax.all_gather(space_shard, 'tm'), axis=0)]
  transfers between devices with their start and end apart: 8 -> 8, of which waited for: 5 -> 4; matrix products, arithmetic and copies ran while one was open for 2% -> 2% of each run, Pallas kernels for 0% -> 0%
where the time goes in v1:
time: 219 us; the launch traced here: 218 us
  blocking collectives  122 us (56%)
  waiting for transfers between devices  54.8 us (25%)
  between operations  14.5 us (7%)
  starting transfers between devices  12.6 us (6%)
  other arithmetic  7.62 us (3%)
  local copies, waits for them, and re-layouts  4.12 us (2%)
    reduce_scatter x1, waiting for transfers between devices, shards(): lax.psum_scatter(local_grad, 'space', scatter_dimension=0, tiled=True)  47.5 us
    psum x1, blocking collectives, shards(): lax.psum(jnp.sum(values, axis=(0, 1, 2, 4)), ('tm', 'space')) / group_count  43.2 us
    psum x1, blocking collectives, shards(): lax.psum(jnp.sum(centered * centered, axis=(0, 1, 2, 4)), ('tm', 'space'))  41 us
    psum x1, blocking collectives, shards(): lax.psum((jnp.sum(activation_grad * normed, axis=(0, 1, 2)), jnp.sum(acti...  38.1 us
    ppermute x4, starting transfers between devices, shifted(): lax.ppermute(value, axis, [(source, source + steps) for source in range(l...  9.8 us
    ppermute x1, waiting for transfers between devices, extended_2(): lax.ppermute(lax.slice_in_dim(block, 0, width, axis=dim), axis, backward)  4.55 us
  transfers between devices with their start and end apart: 8, of which 4 were waited for; matrix products, arithmetic and copies ran while one was open for 2% of the time, Pallas kernels for 0%

profile of v1, /device:TPU:0, one launch (start us, length us, event | category | flops | bytes accessed | tf_op | source)
XLA Modules:
  0.0 218.0 jit_solution(15247144118623093506)
XLA Ops:
  7.2 0.9 convert_reduce_fusion
  8.1 0.1 reduce_sum.78
  8.2 0.1 reduce_sum.79
  8.3 1.3 collective-permute-start
  9.6 43.2 %psum.28 = f32[32]{0:T(128)S(1)} all-reduce(f32[32]{0:T(128)S(1)} %reduce_sum.79), channel_id=1, replica_groups=mesh['tm'=4,'space'=8] {'tm','space'}, use_global_device_ids=true, to_apply=%region_2.0 | all-reduce | flops 32 | bytes 256 | tf_op jit(solution)/shard_map/psum | solution.py:72
  52.8 0.1 sub.35
  52.8 0.1 sub.36
  52.9 0.9 fusion.33
  53.8 0.1 reduce_sum.81
  53.9 0.1 reduce_sum.82
  54.0 1.5 fusion.40
  55.6 41.0 %psum.29 = f32[32]{0:T(128)S(1)} all-reduce(f32[32]{0:T(128)S(1)} %reduce_sum.82), channel_id=1, replica_groups=mesh['tm'=4,'space'=8] {'tm','space'}, use_global_device_ids=true, to_apply=%region_5.6 | all-reduce | flops 32 | bytes 256 | tf_op jit(solution)/shard_map/psum | solution.py:75
  96.6 0.2 copy.15
  96.8 0.2 copy.13
  97.1 0.2 copy.14
  97.4 0.1 constant_dynamic-update-slice_fusion.25
  97.6 0.1 constant_dynamic-update-slice_fusion.23
  97.7 0.1 constant_dynamic-update-slice_fusion.22
  97.8 0.1 constant_dynamic-update-slice_fusion.20
  97.9 0.1 constant_dynamic-update-slice_fusion.19
  98.0 0.3 fusion.42
  98.4 0.3 convolution_add_fusion.1
  98.8 0.3 convolution_add_fusion
  99.2 1.3 collective-permute-start.1
  100.5 0.1 mul.76
  100.6 3.0 %collective-permute-start.2 = (f32[2,32,256]{2,1,0:T(8,128)S(1)}, f32[2,32,256]{2,1,0:T(8,128)S(1)}, u32[]{:S(2)}, u32[]{:S(2)}) collective-permute-start(f32[2,32,256]{2,1,0:T(8,128)S(1)} %get-tuple-element.53), channel_id=1, source_target_pairs={{0,1},{1,2},{2,3},{3,4},{4,5},{5,6},{6,7},{8,9},{9,10},{10,11},{11... | collective-permute-start | bytes 196616 | tf_op jit(solution)/shard_map/ppermute | solution.py:12
  103.7 0.9 collective-permute-done.2
  104.6 0.1 fusion.38
  104.7 4.2 %collective-permute-start.3 = (bf16[2,2,32,256]{3,2,1,0:T(8,128)(2,1)S(1)}, bf16[2,2,32,256]{3,2,1,0:T(8,128)(2,1)S(1)}, u32[]{:S(2)}, u32[]{:S(2)}) collective-permute-start(bf16[2,2,32,256]{3,2,1,0:T(8,128)(2,1)S(1)} %get-tuple-element.90), channel_id=1, source_target_pairs={{0,8},{8,16},{16,24},{1,9},{9,17},{17,25},{2,10},{10,18},{18,26},{... | collective-permute-start | bytes 196616 | tf_op jit(solution)/shard_map/ppermute | solution.py:12
  108.9 1.9 collective-permute-done.3
  110.9 1.4 collective-permute-start.4
  112.3 1.3 collective-permute-start.5
  113.6 4.6 %collective-permute-done.5 = bf16[4,1,32,256]{3,2,1,0:T(8,128)(2,1)S(1)} collective-permute-done((bf16[4,1,32,256]{3,2,1,0:T(8,128)(2,1)S(1)}, bf16[4,1,32,256]{3,2,1,0:T(8,128)(2,1)S(1)}, u32[]{:S(2)}, u32[]{:S(2)}) %collective-permute-start.5) | collective-permute-done | bytes 65568 | tf_op jit(solution)/shard_map/ppermute | solution.py:23
  118.2 0.1 select_maximum_fusion
  118.7 0.3 convolution_bitcast_fusion
  119.0 0.3 convolution_bitcast_fusion.2
  119.4 0.3 convolution_bitcast_fusion.1
  119.7 2.0 pad_maximum_fusion
  121.8 47.5 %reduce-scatter.2.cloned.1.call-done = f32[864,128]{1,0:T(8,128)} async-done(((f32[6912,128]{1,0:T(8,128)}), f32[864,128]{1,0:T(8,128)}) %reduce-scatter.2.cloned.1.call-update) | async-done | bytes 442384 | tf_op jit(solution)/shard_map/reduce_scatter | solution.py:100
  169.3 38.1 %all-reduce.2 = (f32[256]{0:T(256)S(1)}, f32[256]{0:T(256)S(1)}) all-reduce(f32[256]{0:T(256)S(1)} %get-tuple-element.29, f32[256]{0:T(256)S(1)} %get-tuple-element.28), channel_id=1, replica_groups=mesh['tm'=4,'space'=8] {'tm','space'}, use_global_device_ids=true, to_apply=%region_10.11 | all-reduce | flops 512 | bytes 4096 | tf_op jit(solution)/shard_map/psum | solution.py:110
  207.4 0.1 reshape.151
  207.4 0.1 reduce_sum.84
  207.6 0.1 sub.41
  207.7 0.1 reshape.152
  207.8 0.1 reduce_sum.86
  208.0 0.1 mul.89
  208.1 0.7 fusion.32
  208.8 2.4 %reduce_sum.87 = f32[864,128]{1,0:T(8,128)} reduce(f32[4,864,128]{2,1,0:T(8,128)} %bitcast.59, f32[]{:T(128)} %constant.67.clone.1), dimensions={0}, to_apply=%region_13.14 | reduce | flops 331776 | bytes 2211844 | tf_op jit(solution)/shard_map/reduce_sum | solution.py:101
  (51 shorter events, 0.9 us)
Async XLA Ops:
  7.2 162.1 %reduce-scatter.2.cloned.1.call-start = ((), (), s32[]{:S(2)}) async-start(), calls=%async_computation.1 | async-start | bytes 3981312 | tf_op jit(solution)/shard_map/reduce_scatter | solution.py:100
  8.3 89.0 %collective-permute-start = (bf16[2,2,32,128]{3,2,1,0:T(8,128)(2,1)}, bf16[2,2,32,128]{3,2,1,0:T(8,128)(2,1)S(1)}, u32[]{:S(2)}, u32[]{:S(2)}) collective-permute-start(bf16[2,2,32,128]{3,2,1,0:T(8,128)(2,1)} %param.10), channel_id=1, source_target_pairs={{8,0},{16,8},{24,16},{9,1},{17,9},{25,17},{10,2},{18,10},{26,18},{... | collective-permute-start | bytes 98312 | tf_op jit(solution)/shard_map/ppermute | solution.py:12
  96.6 0.8 copy-start.1
  98.4 6.2 %copy-start = (bf16[2,2,32,256]{3,2,1,0:T(8,128)(2,1)S(1)}, bf16[2,2,32,256]{3,2,1,0:T(8,128)(2,1)}, u32[]{:S(2)}) copy-start(bf16[2,2,32,256]{3,2,1,0:T(8,128)(2,1)} %param.9) | copy-start | bytes 196612
  98.4 6.2 %copy-start.2 = (f32[256]{0:T(256)S(1)}, f32[256]{0:T(256)}, u32[]{:S(2)}) copy-start(f32[256]{0:T(256)} %param.12) | copy-start | bytes 3076
  98.4 6.2 %copy-start.3 = (f32[256]{0:T(256)S(1)}, f32[256]{0:T(256)}, u32[]{:S(2)}) copy-start(f32[256]{0:T(256)} %param.13) | copy-start | bytes 3076
  99.2 4.5 %collective-permute-start.1 = (f32[2,32,256]{2,1,0:T(8,128)S(1)}, f32[2,32,256]{2,1,0:T(8,128)S(1)}, u32[]{:S(2)}, u32[]{:S(2)}) collective-permute-start(f32[2,32,256]{2,1,0:T(8,128)S(1)} %get-tuple-element.54), channel_id=1, source_target_pairs={{1,0},{2,1},{3,2},{4,3},{5,4},{6,5},{7,6},{9,8},{10,9},{11,10},{12... | collective-permute-start | bytes 196616 | tf_op jit(solution)/shard_map/ppermute | solution.py:12
  100.6 3.9 %collective-permute-start.2 = (f32[2,32,256]{2,1,0:T(8,128)S(1)}, f32[2,32,256]{2,1,0:T(8,128)S(1)}, u32[]{:S(2)}, u32[]{:S(2)}) collective-permute-start(f32[2,32,256]{2,1,0:T(8,128)S(1)} %get-tuple-element.53), channel_id=1, source_target_pairs={{0,1},{1,2},{2,3},{3,4},{4,5},{5,6},{6,7},{8,9},{9,10},{10,11},{11... | collective-permute-start | bytes 196616 | tf_op jit(solution)/shard_map/ppermute | solution.py:12
  104.7 6.1 %collective-permute-start.3 = (bf16[2,2,32,256]{3,2,1,0:T(8,128)(2,1)S(1)}, bf16[2,2,32,256]{3,2,1,0:T(8,128)(2,1)S(1)}, u32[]{:S(2)}, u32[]{:S(2)}) collective-permute-start(bf16[2,2,32,256]{3,2,1,0:T(8,128)(2,1)S(1)} %get-tuple-element.90), channel_id=1, source_target_pairs={{0,8},{8,16},{16,24},{1,9},{9,17},{17,25},{2,10},{10,18},{18,26},{... | collective-permute-start | bytes 196616 | tf_op jit(solution)/shard_map/ppermute | solution.py:12
  110.9 2.8 %collective-permute-start.4 = (bf16[4,1,32,256]{3,2,1,0:T(8,128)(2,1)S(1)}, bf16[4,1,32,256]{3,2,1,0:T(8,128)(2,1)S(1)}, u32[]{:S(2)}, u32[]{:S(2)}) collective-permute-start(bf16[4,1,32,256]{3,2,1,0:T(8,128)(2,1)S(1)} %get-tuple-element.88), channel_id=1, source_target_pairs={{0,1},{1,2},{2,3},{3,4},{4,5},{5,6},{6,7},{8,9},{9,10},{10,11},{11... | collective-permute-start | bytes 196616 | tf_op jit(solution)/shard_map/ppermute | solution.py:20
  112.3 5.9 %collective-permute-start.5 = (bf16[4,1,32,256]{3,2,1,0:T(8,128)(2,1)S(1)}, bf16[4,1,32,256]{3,2,1,0:T(8,128)(2,1)S(1)}, u32[]{:S(2)}, u32[]{:S(2)}) collective-permute-start(bf16[4,1,32,256]{3,2,1,0:T(8,128)(2,1)S(1)} %get-tuple-element.89), channel_id=1, source_target_pairs={{1,0},{2,1},{3,2},{4,3},{5,4},{6,5},{7,6},{9,8},{10,9},{11,10},{12... | collective-permute-start | bytes 196616 | tf_op jit(solution)/shard_map/ppermute | solution.py:23
  121.7 87.1 %all-gather.3.cloned.1.call-start = ((), (), s32[]{:S(2)}) async-start(), calls=%async_computation.2 | async-start | bytes 2211840 | tf_op jit(solution)/shard_map/all_gather | solution.py:101
  207.3 3.8 %copy-start.4 = (f32[256]{0:T(256)}, f32[256]{0:T(256)S(1)}, u32[]{:S(2)}) copy-start(f32[256]{0:T(256)S(1)} %get-tuple-element.30) | copy-start | bytes 3076
  207.3 3.8 %copy-start.5 = (f32[256]{0:T(256)}, f32[256]{0:T(256)S(1)}, u32[]{:S(2)}) copy-start(f32[256]{0:T(256)S(1)} %get-tuple-element.31) | copy-start | bytes 3076
Sparse Core Ops, SparseCore 0:
  121.8 47.3 reduce-scatter.1
  171.2 31.3 all-gather.2
